TPU v7x, 128 devices: a whole 4x4x4 slice. The times are simulated.
128 devices in a mesh: row: 8 (over y, z_hi), col: 16 (over x, z_lo, core).
Axes of the slice: x: 4, y: 4, z: 4 (z_hi: 2, z_lo: 2; z = z_hi * 2 + z_lo), core: 2. Of those that a mesh axis runs over, the one named last changes fastest.
Arguments:
- tokens: bfloat16 [16448, 1024], P('row', 'col'), may hold values from -6 to 6
- qkv_weight: bfloat16 [1024, 3072], P('col', 'row'), may hold values from -2 to 2
- persistent: bfloat16 [16, 2, 1024], P(None, None, 'row'), may hold values from -6 to 6
- cache_pages: bfloat16 [1024, 256, 2, 1024], P('col', None, None, 'row'), may hold values from -48 to 48
- page_table: int32 [64, 16], P('col'), may hold values from 0 to 63, as said below
- cache_len: int32 [64], P('col'), may hold values from 1 to 4096, as said below
- destination: int32 [16], P('col'), may hold values from 0 to 15, each once
- memory_in: float32 [16, 8, 128, 128], P('col', 'row'), may hold values from -6 to 6
- momentum_in: float32 [16, 8, 128, 128], P('col', 'row'), may hold values from -3 to 3
- forget_rate: float32 [16, 8, 16], P('col', 'row'), may hold values from 0.02 to 0.5
- keep_rate: float32 [16, 8, 16], P('col', 'row'), may hold values from 0.3 to 0.95
- learn_rate: float32 [16, 8, 16], P('col', 'row'), may hold values from 0.05 to 1
- decode_memory: float32 [64, 8, 128, 128], P('col', 'row'), may hold values from -6 to 6
Outputs:
- heads_out: bfloat16 [16448, 1024], P('col', 'row')
- memory_out: float32 [16, 8, 128, 128], P('col', 'row')
- momentum_out: float32 [16, 8, 128, 128], P('col', 'row')
Inputs may be any that keep to these rules, and one draw needn't show every extreme that they name: `page_table`: the 4 decode requests of one index of col together name every page of that index's pool once. `cache_len`: some request has exactly 4096. `destination`: each request block once.
All inputs are finite; a program needn't handle non-finite values.
Results may differ from a plain program's by a relative error of at most 0.012.
The roundings to bfloat16 on the way count: a program that leaves them out, or rounds other values in their place, can miss the bound.
Values may be sent and summed in bfloat16 or wider, within the bound.
No kernel may reach another device: no remote copies, remote signals or barrier semaphores. Data moves between devices by JAX's collectives and lax.ppermute only.
A program may use at most 128 MiB of HBM per device.

v0:
```python
import jax
import jax.numpy as jnp
from jax import lax
from jax.sharding import PartitionSpec as P

HD = 128
PERS = 16
MCH = 64
PCH = 1024
DEC_DEV = 4
CACHE = 4096
epsilon = 1e-06
highest = lax.Precision.HIGHEST


def unit_rows(values):
    return values / jnp.sqrt(jnp.sum(values * values, axis=-1, keepdims=True) + epsilon)


def memory_spans(
    query_unit, key_unit, value_rows, memory, momentum, forget_rate, keep_rate, learn_rate
):

    def advance(carry, inputs):
        memory_now, momentum_now = carry
        query_now, key_now, value_now, forget_now, keep_now, learn_now = inputs
        readout = jnp.dot(query_now, memory_now, precision=highest)
        errors = jnp.dot(key_now, memory_now, precision=highest) - value_now
        gradient = jnp.dot(key_now.T, errors, precision=highest) * (2.0 / MCH)
        momentum_now = keep_now * momentum_now - learn_now * gradient
        memory_now = (1.0 - forget_now) * memory_now + momentum_now
        return ((memory_now, momentum_now), readout)

    (memory, momentum), readouts = lax.scan(
        advance,
        (memory, momentum),
        (query_unit, key_unit, value_rows, forget_rate, keep_rate, learn_rate),
    )
    return (readouts, memory, momentum)


def window_attention(query_rows, key_rows, value_rows, persist_key, persist_value):
    scale_factor = query_rows.shape[-1] ** (-0.5)
    inner_score = (
        jnp.einsum("nqd,nkd->nqk", query_rows, key_rows, preferred_element_type=jnp.float32)
        * scale_factor
    )
    length_q = query_rows.shape[1]
    causal = jnp.arange(length_q)[:, None] >= jnp.arange(length_q)[None, :]
    inner_score = jnp.where(causal[None], inner_score, -jnp.inf)
    outer_score = (
        jnp.einsum("nqd,pd->nqp", query_rows, persist_key, preferred_element_type=jnp.float32)
        * scale_factor
    )
    highest_score = jnp.maximum(jnp.max(inner_score, axis=-1), jnp.max(outer_score, axis=-1))[
        ..., None
    ]
    inner_exp = jnp.exp(inner_score - highest_score)
    outer_exp = jnp.exp(outer_score - highest_score)
    totals = jnp.sum(inner_exp, axis=-1, keepdims=True) + jnp.sum(outer_exp, axis=-1, keepdims=True)
    inner_weight = (inner_exp / totals).astype(jnp.bfloat16)
    outer_weight = (outer_exp / totals).astype(jnp.bfloat16)
    attended = jnp.einsum(
        "nqk,nkd->nqd", inner_weight, value_rows, preferred_element_type=jnp.float32
    )
    return attended + jnp.einsum(
        "nqp,pd->nqd", outer_weight, persist_value, preferred_element_type=jnp.float32
    )


def prefill_head(
    token_block, persist_key, persist_value, memory, momentum, forget_rate, keep_rate, learn_rate
):
    spans = token_block.shape[0] // MCH
    query_rows = token_block[:, 0].reshape(spans, MCH, -1)
    key_rows = token_block[:, 1].reshape(spans, MCH, -1)
    value_rows = token_block[:, 2].reshape(spans, MCH, -1)
    readouts, memory, momentum = memory_spans(
        unit_rows(query_rows.astype(jnp.float32)),
        unit_rows(key_rows.astype(jnp.float32)),
        value_rows.astype(jnp.float32),
        memory,
        momentum,
        forget_rate,
        keep_rate,
        learn_rate,
    )
    attended = window_attention(query_rows, key_rows, value_rows, persist_key, persist_value)
    return (
        (attended + readouts).reshape(-1, token_block.shape[-1]).astype(jnp.bfloat16),
        memory,
        momentum,
    )


def decode_block(row_block, cache_block, persist_key, persist_value, memory_now, length_now):
    scale_factor = row_block.shape[-1] ** (-0.5)
    query_row = row_block[:, 0]
    key_row = row_block[:, 1]
    value_row = row_block[:, 2]
    cache_score = (
        jnp.einsum("chd,hd->hc", cache_block[:, 0], query_row, preferred_element_type=jnp.float32)
        * scale_factor
    )
    live_mask = jnp.arange(cache_block.shape[0]) < length_now
    cache_score = jnp.where(live_mask[None, :], cache_score, -jnp.inf)
    own_score = (
        jnp.sum(query_row.astype(jnp.float32) * key_row.astype(jnp.float32), axis=-1) * scale_factor
    )
    persist_score = (
        jnp.einsum("phd,hd->hp", persist_key, query_row, preferred_element_type=jnp.float32)
        * scale_factor
    )
    highest_score = jnp.maximum(
        jnp.maximum(jnp.max(cache_score, axis=-1), own_score), jnp.max(persist_score, axis=-1)
    )
    cache_exp = jnp.exp(cache_score - highest_score[:, None])
    own_exp = jnp.exp(own_score - highest_score)
    persist_exp = jnp.exp(persist_score - highest_score[:, None])
    totals = jnp.sum(cache_exp, axis=-1) + own_exp + jnp.sum(persist_exp, axis=-1)
    cache_weight = (cache_exp / totals[:, None]).astype(jnp.bfloat16)
    own_weight = (own_exp / totals).astype(jnp.bfloat16)
    persist_weight = (persist_exp / totals[:, None]).astype(jnp.bfloat16)
    attended = jnp.einsum(
        "hc,chd->hd", cache_weight, cache_block[:, 1], preferred_element_type=jnp.float32
    )
    attended = attended + own_weight.astype(jnp.float32)[:, None] * value_row.astype(jnp.float32)
    attended = attended + jnp.einsum(
        "hp,phd->hd", persist_weight, persist_value, preferred_element_type=jnp.float32
    )
    readout = jnp.einsum(
        "hd,hde->he", unit_rows(query_row.astype(jnp.float32)), memory_now, precision=highest
    )
    return (attended + readout).astype(jnp.bfloat16)


def shards(
    tokens,
    qkv_weight,
    persistent,
    cache_pages,
    page_table,
    cache_len,
    destination,
    memory_in,
    momentum_in,
    forget_rate,
    keep_rate,
    learn_rate,
    decode_memory,
):
    block_rows = PCH + DEC_DEV
    heads_dev = qkv_weight.shape[1] // (3 * HD)
    gathered = lax.all_gather(tokens, "row", axis=0, tiled=True)
    projected = lax.psum_scatter(
        jnp.dot(gathered, qkv_weight, preferred_element_type=jnp.float32),
        "col",
        scatter_dimension=0,
        tiled=True,
    )
    projected = projected.astype(jnp.bfloat16).reshape(block_rows, heads_dev, 3, HD)
    slot_count = lax.axis_size("col")
    target = (jnp.arange(slot_count, dtype=jnp.int32) == destination[0]).astype(jnp.float32)
    states = jnp.stack([memory_in[0], momentum_in[0]], axis=0)
    outgoing = target[:, None, None, None, None] * states[None]
    arrived = jnp.sum(
        lax.all_to_all(outgoing, "col", split_axis=0, concat_axis=0, tiled=True), axis=0
    )
    persist = persistent.reshape(PERS, 2, heads_dev, HD)
    out_rows, memory_next, momentum_next = prefill_head(
        projected[:PCH, 0],
        persist[:, 0, 0],
        persist[:, 1, 0],
        arrived[0, 0],
        arrived[1, 0],
        forget_rate[0, 0],
        keep_rate[0, 0],
        learn_rate[0, 0],
    )
    prefill_list = [out_rows]
    memory_list = [memory_next]
    momentum_list = [momentum_next]
    caches = cache_pages[page_table.reshape(-1)].reshape(DEC_DEV, CACHE, 2, heads_dev, HD)
    decode_map = jax.vmap(decode_block, in_axes=(0, 0, None, None, 0, 0))
    decode_out = decode_map(
        projected[PCH:], caches, persist[:, 0], persist[:, 1], decode_memory, cache_len
    )
    prefill_out = jnp.stack(prefill_list, axis=1)
    heads_out = jnp.concatenate([prefill_out, decode_out], axis=0).reshape(
        block_rows, heads_dev * HD
    )
    return (heads_out, jnp.stack(memory_list, axis=0)[None], jnp.stack(momentum_list, axis=0)[None])


def solution(mesh):
    placed = (
        P("row", "col"),
        P("col", "row"),
        P(None, None, "row"),
        P("col", None, None, "row"),
        P("col", None),
        P("col"),
        P("col"),
        P("col", "row", None, None),
        P("col", "row", None, None),
        P("col", "row", None),
        P("col", "row", None),
        P("col", "row", None),
        P("col", "row", None, None),
    )
    return jax.shard_map(
        shards,
        mesh=mesh,
        in_specs=placed,
        out_specs=(P("col", "row"), P("col", "row", None, None), P("col", "row", None, None)),
        check_vma=False,
    )
```

profile of v0, /device:TPU:1, one launch (start us, length us, event | category | flops | bytes accessed | tf_op | source)
XLA Modules:
  0.0 477.1 jit_solution(6140073066499957147)
XLA Ops:
  7.2 0.7 all-gather.3.cloned.1.call-update
  8.6 0.9 maximum_bitcast_fusion.1
  9.5 1.6 broadcast_multiply_fusion
  11.1 7.2 %all-to-all-start = ((f32[16,2,1,128,128]{4,3,2,1,0:T(8,128)}), f32[16,2,1,128,128]{4,3,2,1,0:T(8,128)S(1)}, u32[]{:S(2)}, u32[]{:S(2)}) async-start(f32[16,2,1,128,128]{4,3,2,1,0:T(8,128)} %broadcast_multiply_fusion), calls=%async_computation | async-start | bytes 4194304 | tf_op jit(solution)/shard_map/all_to_all | solution.py:167
  18.4 22.1 %gather_fusion = bf16[64,256,2,128]{3,2,1,0:T(2,128)(2,1)} fusion(bf16[64,256,2,128]{3,2,1,0:T(2,128)(2,1)} %param.18, s32[1024]{0:T(1024)S(1)} %pad_clamp_fusion), kind=kCustom, calls=%fused_computation | custom fusion | bytes 16777472 | tf_op jit(solution)/shard_map/gather | solution.py:183
  40.5 8.8 %copy.43 = bf16[64,256,2,128]{3,1,0,2:T(8,128)(2,1)} copy(bf16[64,256,2,128]{3,2,1,0:T(2,128)(2,1)} %gather_fusion) | data formatting | bytes 16777216 | tf_op jit(solution)/shard_map/gather | solution.py:183
  50.7 34.3 %all-gather.3.cloned.1.call-done = bf16[8,2056,64]{1,2,0:T(8,128)(2,1)} async-done(((bf16[1,2056,64]{1,2,0:T(8,128)(2,1)}), bf16[8,2056,64]{1,2,0:T(8,128)(2,1)}) %all-gather.3.cloned.1.call-update) | async-done | bytes 2105360 | tf_op jit(solution)/shard_map/all_gather | solution.py:154
  85.0 2.9 copy.36
  87.9 3.0 reshape.345
  90.9 13.4 %fusion.56 = f32[16448,384]{1,0:T(8,128)} fusion(bf16[16448,64]{0,1:T(8,128)(2,1)} %reshape.345, bf16[64,384]{1,0:T(8,128)(2,1)S(1)} %copy-done.4), kind=kOutput, calls=%fused_computation.104 | convolution fusion | flops 808452096 | bytes 27418624 | tf_op jit(solution)/shard_map/dot_general | solution.py:156
  104.3 271.0 %fusion = f32[1040,384]{1,0:T(8,128)S(1)} fusion(f32[16448,384]{1,0:T(8,128)} %fusion.56), kind=kCustom, calls=%all-reduce-scatter | all-reduce-scatter fusion | flops 6389761 | bytes 26862080
  375.3 4.6 collective-permute-start
  379.9 1.8 collective-permute-done
  381.7 2.1 concatenate.4
  386.8 1.1 fusion.23
  388.5 73.0 %while.14 = (s32[]{:T(128)}, f32[128,128]{1,0:T(8,128)S(1)}, f32[128,128]{1,0:T(8,128)S(1)}, f32[16,64,128]{2,1,0:T(8,128)S(1)}, f32[16]{0:T(128)S(1)}, /*index=...) while((s32[]{:T(128)}, f32[128,128]{1,0:T(8,128)S(1)}, ...), condition=%wide.region_9.10_spmd, body=%wide.region_8.9_spmd.sunk | while | flops 37838852 | bytes 624841 | solution.py:34
  391.4 0.7 dynamic_slice.48
  392.1 1.0 multiply_add_fusion.2
  396.0 0.7 dynamic_slice.48
  396.7 1.0 multiply_add_fusion.2
  400.5 0.7 dynamic_slice.48
  401.2 1.0 multiply_add_fusion.2
  405.1 0.7 dynamic_slice.48
  405.8 1.0 multiply_add_fusion.2
  409.7 0.7 dynamic_slice.48
  410.3 1.0 multiply_add_fusion.2
  414.2 0.7 dynamic_slice.48
  414.9 1.0 multiply_add_fusion.2
  418.8 0.7 dynamic_slice.48
  419.5 1.0 multiply_add_fusion.2
  423.4 0.7 dynamic_slice.48
  424.0 1.0 multiply_add_fusion.2
  427.9 0.7 dynamic_slice.48
  428.6 1.0 multiply_add_fusion.2
  432.5 0.7 dynamic_slice.48
  433.2 1.0 multiply_add_fusion.2
  437.7 1.0 multiply_add_fusion.2
  442.3 1.0 multiply_add_fusion.2
  446.8 1.0 multiply_add_fusion.2
  450.7 0.7 dynamic_slice.48
  451.4 1.0 multiply_add_fusion.2
  455.3 0.7 dynamic_slice.48
  456.0 1.0 multiply_add_fusion.2
  459.9 0.7 dynamic_slice.48
  460.5 1.0 multiply_add_fusion.2
  461.6 3.4 fusion.13
  465.8 2.8 fusion.12
  469.5 0.7 maximum_bitcast_fusion
  (140 shorter events, 32.7 us)
Async XLA Ops:
  7.2 461.9 %copy-start = (f32[4,1,128,128]{3,2,1,0:T(8,128)S(1)}, f32[4,1,128,128]{3,2,1,0:T(8,128)}, u32[]{:S(2)}) copy-start(f32[4,1,128,128]{3,2,1,0:T(8,128)} %param.27) | copy-start | bytes 786436
  7.2 11.1 %copy-start.5 = (bf16[16,2,128]{2,1,0:T(2,128)(2,1)S(1)}, bf16[16,2,128]{2,1,0:T(2,128)(2,1)}, u32[]{:S(2)}) copy-start(bf16[16,2,128]{2,1,0:T(2,128)(2,1)} %param.17) | copy-start | bytes 24580
  7.2 11.1 %copy-start.6 = (s32[4,16]{1,0:T(4,128)S(1)}, s32[4,16]{1,0:T(4,128)}, u32[]{:S(2)}) copy-start(s32[4,16]{1,0:T(4,128)} %param.19) | copy-start | bytes 772
  7.2 77.8 %all-gather.3.cloned.1.call-start = ((), (), s32[]{:S(2)}) async-start(), calls=%async_computation.1 | async-start | bytes 2506752 | tf_op jit(solution)/shard_map/all_gather | solution.py:154
  11.1 39.5 %all-to-all-start = ((f32[16,2,1,128,128]{4,3,2,1,0:T(8,128)}), f32[16,2,1,128,128]{4,3,2,1,0:T(8,128)S(1)}, u32[]{:S(2)}, u32[]{:S(2)}) async-start(f32[16,2,1,128,128]{4,3,2,1,0:T(8,128)} %broadcast_multiply_fusion), calls=%async_computation | async-start | bytes 4194304 | tf_op jit(solution)/shard_map/all_to_all | solution.py:167
  40.5 8.8 %copy-start.8 = (u32[128]{0:T(128)S(1)}, u32[128]{0:T(128)}, u32[]{:S(2)}) copy-start(u32[128]{0:T(128)} %constant.47) | copy-start | bytes 1540
  50.7 40.2 %copy-start.4 = (bf16[64,384]{1,0:T(8,128)(2,1)S(1)}, bf16[64,384]{1,0:T(8,128)(2,1)}, u32[]{:S(2)}) copy-start(bf16[64,384]{1,0:T(8,128)(2,1)} %param.16) | copy-start | bytes 147460
  375.3 6.4 %collective-permute-start = (bf16[180,384]{1,0:T(8,128)(2,1)S(1)}, bf16[180,384]{1,0:T(8,128)(2,1)}, u32[]{:S(2)}, u32[]{:S(2)}) collective-permute-start(bf16[180,384]{1,0:T(8,128)(2,1)S(1)} %slice.81), channel_id=1, source_target_pairs={{0,1},{1,2},{2,3},{3,4},{4,5},{5,6},{6,7},{7,8},{8,9},{9,10},{10,1... | collective-permute-start | bytes 414728
  385.2 3.3 copy-start.9
  385.2 3.3 copy-start.10
  385.2 3.3 copy-start.11
  388.5 76.5 %copy-start.7 = (s32[4]{0:T(128)S(1)}, s32[4]{0:T(128)}, u32[]{:S(2)}) copy-start(s32[4]{0:T(128)} %param.20) | copy-start | bytes 52
  461.5 7.1 %copy-start.1 = (f32[128,128]{1,0:T(8,128)}, f32[128,128]{1,0:T(8,128)S(1)}, u32[]{:S(2)}) copy-start(f32[128,128]{1,0:T(8,128)S(1)} %get-tuple-element.58) | copy-start | bytes 196612
  461.6 7.1 %copy-start.2 = (f32[128,128]{1,0:T(8,128)}, f32[128,128]{1,0:T(8,128)S(1)}, u32[]{:S(2)}) copy-start(f32[128,128]{1,0:T(8,128)S(1)} %get-tuple-element.59) | copy-start | bytes 196612
  461.6 7.1 %copy-start.3 = (f32[16,64,128]{2,1,0:T(8,128)S(1)}, f32[16,64,128]{2,1,0:T(8,128)}, u32[]{:S(2)}) copy-start(f32[16,64,128]{2,1,0:T(8,128)} %fusion.23) | copy-start | bytes 1572868
Sparse Core Ops, SparseCore 0:
  10.3 74.6 all-gather.2
where the time goes:
time: 478 us; the launch traced here: 477 us
  blocking collectives  271 us (57%)
  local copies, waits for them, and re-layouts  70.9 us (15%)
  matrix products  44.4 us (9%)
  waiting for transfers between devices  36.8 us (8%)
  loops' own time  21.4 us (4%)
  between operations  15.7 us (3%)
  starting transfers between devices  11.8 us (2%)
  other arithmetic  5.13 us (1%)
    unnamed x1, blocking collectives  271 us
    all_gather x1, waiting for transfers between devices, shards(): gathered = lax.all_gather(tokens, 'row', axis=0, tiled=True)  34.3 us
    gather x2, local copies, waits for them, and re-layouts, shards(): cache_pages[page_table.reshape(-1)]  30.9 us
    dynamic_slice x48, local copies, waits for them, and re-layouts, memory_spans(): lax.scan(advance, (memory, momentum), (query_unit, key_unit, value_rows,...  29.6 us
    another operation x1, loops' own time, memory_spans(): lax.scan(advance, (memory, momentum), (query_unit, key_unit, value_rows,...  21.4 us
    dot_general x16, matrix products, advance(): gradient = jnp.dot(key_now.T, errors, precision=highest) * (2.0 / MCH)  16 us
    dot_general x1, matrix products, shards(): jnp.dot(gathered, qkv_weight, preferred_element_type=jnp.float32)  13.4 us
  transfers between devices with their start and end apart: 3, of which 2 were waited for; matrix products, arithmetic and copies ran while one was open for 7% of the time, Pallas kernels for 0%

commit v1 on v0

--- a/solution.py
+++ b/solution.py
@@ -151,7 +151,9 @@
 ):
     block_rows = PCH + DEC_DEV
     heads_dev = qkv_weight.shape[1] // (3 * HD)
-    gathered = lax.all_gather(tokens, "row", axis=0, tiled=True)
+    gathered = jnp.concatenate(
+        lax.all_to_all(jnp.stack([tokens] * lax.axis_size("row")), "row", 0, 0), axis=0
+    )
     projected = lax.psum_scatter(
         jnp.dot(gathered, qkv_weight, preferred_element_type=jnp.float32),
         "col",

time: 478 us -> 438 us (0.916)
  waiting for transfers between devices: 36.8 us -> 0.1 us
  between operations: 15.7 us -> 2.37 us
  starting transfers between devices: 11.8 us -> 18.6 us
    all_gather x1 -> x0, waiting for transfers between devices: 34.3 us -> none  [shards(): gathered = lax.all_gather(tokens, 'row', axis=0, tiled=True)]
    all_to_all x0 -> x1, starting transfers between devices: none -> 8.33 us  [shards(): lax.all_to_all(jnp.stack([tokens] * lax.axis_size('row')), 'row', 0, 0)]
  transfers between devices with their start and end apart: 3 -> 3, of which waited for: 2 -> 1; matrix products, arithmetic and copies ran while one was open for 7% -> 74% of each run, Pallas kernels for 0% -> 0%
where the time goes in v1:
time: 438 us; the launch traced here: 437 us
  blocking collectives  273 us (62%)
  local copies, waits for them, and re-layouts  74 us (17%)
  matrix products  41.1 us (9%)
  loops' own time  21.4 us (5%)
  starting transfers between devices  18.6 us (4%)
  other arithmetic  5.86 us (1%)
    unnamed x1, blocking collectives  273 us
    gather x2, local copies, waits for them, and re-layouts, shards(): cache_pages[page_table.reshape(-1)]  31 us
    dynamic_slice x48, local copies, waits for them, and re-layouts, memory_spans(): lax.scan(advance, (memory, momentum), (query_unit, key_unit, value_rows,...  29.6 us
    another operation x1, loops' own time, memory_spans(): lax.scan(advance, (memory, momentum), (query_unit, key_unit, value_rows,...  21.4 us
    dot_general x16, matrix products, advance(): gradient = jnp.dot(key_now.T, errors, precision=highest) * (2.0 / MCH)  16 us
    dot_general x1, matrix products, shards(): jnp.dot(gathered, qkv_weight, preferred_element_type=jnp.float32)  10.2 us
  transfers between devices with their start and end apart: 3, of which 1 were waited for; matrix products, arithmetic and copies ran while one was open for 74% of the time, Pallas kernels for 0%

profile of v1, /device:TPU:1, one launch (start us, length us, event | category | flops | bytes accessed | tf_op | source)
XLA Modules:
  0.0 436.9 jit_solution(920388106208024397)
XLA Ops:
  0.7 2.7 stack.4
  3.3 8.3 %all-to-all-start = ((bf16[8,2056,64]{1,2,0:T(8,128)(2,1)}), bf16[8,2056,64]{1,2,0:T(8,128)(2,1)S(1)}, u32[]{:S(2)}, u32[]{:S(2)}) async-start(bf16[8,2056,64]{1,2,0:T(8,128)(2,1)} %stack.4), calls=%async_computation | async-start | bytes 4456448 | tf_op jit(solution)/shard_map/all_to_all | solution.py:155
  12.4 22.1 %gather_fusion = bf16[64,256,2,128]{3,2,1,0:T(2,128)(2,1)} fusion(bf16[64,256,2,128]{3,2,1,0:T(2,128)(2,1)} %param.18, s32[1024]{0:T(1024)S(1)} %pad_clamp_fusion), kind=kCustom, calls=%fused_computation | custom fusion | bytes 16777472 | tf_op jit(solution)/shard_map/gather | solution.py:185
  34.6 8.9 %copy.52 = bf16[64,256,2,128]{3,1,0,2:T(8,128)(2,1)} copy(bf16[64,256,2,128]{3,2,1,0:T(2,128)(2,1)} %gather_fusion) | data formatting | bytes 16777216 | tf_op jit(solution)/shard_map/gather | solution.py:185
  44.7 1.6 broadcast_multiply_fusion
  46.3 5.7 %all-to-all-start.1 = ((f32[16,2,1,128,128]{4,3,2,1,0:T(8,128)}), f32[16,2,1,128,128]{4,3,2,1,0:T(8,128)}, u32[]{:S(2)}, u32[]{:S(2)}) async-start(f32[16,2,1,128,128]{4,3,2,1,0:T(8,128)} %broadcast_multiply_fusion), calls=%async_computation.1 | async-start | bytes 4194304 | tf_op jit(solution)/shard_map/all_to_all | solution.py:169
  52.1 2.6 copy.45
  54.7 3.6 reshape.331
  58.4 10.2 %fusion.56 = f32[16448,384]{1,0:T(8,128)} fusion(bf16[16448,64]{0,1:T(8,128)(2,1)S(1)} %reshape.331, bf16[64,384]{1,0:T(8,128)(2,1)S(1)} %copy-done.6), kind=kOutput, calls=%fused_computation.104 | convolution fusion | flops 808452096 | bytes 27418624 | tf_op jit(solution)/shard_map/dot_general | solution.py:158
  68.5 273.4 %fusion = f32[1040,384]{1,0:T(8,128)S(1)} fusion(f32[16448,384]{1,0:T(8,128)} %fusion.56), kind=kCustom, calls=%all-reduce-scatter | all-reduce-scatter fusion | flops 6389761 | bytes 26862080
  342.0 4.6 %collective-permute-start = (bf16[180,384]{1,0:T(8,128)(2,1)S(1)}, bf16[180,384]{1,0:T(8,128)(2,1)}, u32[]{:S(2)}, u32[]{:S(2)}) collective-permute-start(bf16[180,384]{1,0:T(8,128)(2,1)S(1)} %slice.81), channel_id=1, source_target_pairs={{0,1},{1,2},{2,3},{3,4},{4,5},{5,6},{6,7},{7,8},{8,9},{9,10},{10,1... | collective-permute-start | bytes 414728
  346.6 1.7 reduce_sum.83
  348.4 2.1 concatenate.4
  353.5 1.1 fusion.23
  355.2 73.0 %while.14 = (s32[]{:T(128)}, f32[128,128]{1,0:T(8,128)S(1)}, f32[128,128]{1,0:T(8,128)S(1)}, f32[16,64,128]{2,1,0:T(8,128)S(1)}, f32[16]{0:T(128)S(1)}, /*index=...) while((s32[]{:T(128)}, f32[128,128]{1,0:T(8,128)S(1)}, ...), condition=%wide.region_9.10_spmd, body=%wide.region_8.9_spmd.sunk | while | flops 37838852 | bytes 624841 | solution.py:34
  358.1 0.7 dynamic_slice.48
  358.8 1.0 multiply_add_fusion.2
  362.6 0.7 dynamic_slice.48
  363.3 1.0 multiply_add_fusion.2
  367.2 0.7 dynamic_slice.48
  367.9 1.0 multiply_add_fusion.2
  371.8 0.7 dynamic_slice.48
  372.4 1.0 multiply_add_fusion.2
  376.3 0.7 dynamic_slice.48
  377.0 1.0 multiply_add_fusion.2
  380.9 0.7 dynamic_slice.48
  381.6 1.0 multiply_add_fusion.2
  386.1 1.0 multiply_add_fusion.2
  390.0 0.7 dynamic_slice.48
  390.7 1.0 multiply_add_fusion.2
  394.6 0.7 dynamic_slice.48
  395.3 1.0 multiply_add_fusion.2
  399.1 0.7 dynamic_slice.48
  399.8 1.0 multiply_add_fusion.2
  403.7 0.7 dynamic_slice.48
  404.4 1.0 multiply_add_fusion.2
  408.3 0.7 dynamic_slice.48
  408.9 1.0 multiply_add_fusion.2
  412.8 0.7 dynamic_slice.48
  413.5 1.0 multiply_add_fusion.2
  418.1 1.0 multiply_add_fusion.2
  422.0 0.7 dynamic_slice.48
  422.6 1.0 multiply_add_fusion.2
  426.5 0.7 dynamic_slice.48
  427.2 1.0 multiply_add_fusion.2
  428.2 3.4 fusion.13
  432.5 2.8 fusion.12
  436.2 0.7 maximum_bitcast_fusion
  (144 shorter events, 32.0 us)
Async XLA Ops:
  0.6 435.1 %copy-start = (f32[4,1,128,128]{3,2,1,0:T(8,128)S(1)}, f32[4,1,128,128]{3,2,1,0:T(8,128)}, u32[]{:S(2)}) copy-start(f32[4,1,128,128]{3,2,1,0:T(8,128)} %param.27) | copy-start | bytes 786436
  0.6 11.0 %copy-start.7 = (bf16[16,2,128]{2,1,0:T(2,128)(2,1)S(1)}, bf16[16,2,128]{2,1,0:T(2,128)(2,1)}, u32[]{:S(2)}) copy-start(bf16[16,2,128]{2,1,0:T(2,128)(2,1)} %param.17) | copy-start | bytes 24580
  0.7 11.7 %copy-start.8 = (s32[4,16]{1,0:T(4,128)S(1)}, s32[4,16]{1,0:T(4,128)}, u32[]{:S(2)}) copy-start(s32[4,16]{1,0:T(4,128)} %param.19) | copy-start | bytes 772
  3.3 43.0 %all-to-all-start = ((bf16[8,2056,64]{1,2,0:T(8,128)(2,1)}), bf16[8,2056,64]{1,2,0:T(8,128)(2,1)S(1)}, u32[]{:S(2)}, u32[]{:S(2)}) async-start(bf16[8,2056,64]{1,2,0:T(8,128)(2,1)} %stack.4), calls=%async_computation | async-start | bytes 4456448 | tf_op jit(solution)/shard_map/all_to_all | solution.py:155
  34.6 8.9 %copy-start.10 = (u32[128]{0:T(128)S(1)}, u32[128]{0:T(128)}, u32[]{:S(2)}) copy-start(u32[128]{0:T(128)} %constant.47) | copy-start | bytes 1540
  34.6 10.1 %copy-start.4 = (f32[1,1,128,128]{3,2,1,0:T(8,128)S(1)}, f32[1,1,128,128]{3,2,1,0:T(8,128)}, u32[]{:S(2)}) copy-start(f32[1,1,128,128]{3,2,1,0:T(8,128)} %param.23) | copy-start | bytes 196612
  34.6 10.1 %copy-start.5 = (f32[1,1,128,128]{3,2,1,0:T(8,128)S(1)}, f32[1,1,128,128]{3,2,1,0:T(8,128)}, u32[]{:S(2)}) copy-start(f32[1,1,128,128]{3,2,1,0:T(8,128)} %param.22) | copy-start | bytes 196612
  46.3 300.2 %all-to-all-start.1 = ((f32[16,2,1,128,128]{4,3,2,1,0:T(8,128)}), f32[16,2,1,128,128]{4,3,2,1,0:T(8,128)}, u32[]{:S(2)}, u32[]{:S(2)}) async-start(f32[16,2,1,128,128]{4,3,2,1,0:T(8,128)} %broadcast_multiply_fusion), calls=%async_computation.1 | async-start | bytes 4194304 | tf_op jit(solution)/shard_map/all_to_all | solution.py:169
  52.1 6.3 %copy-start.6 = (bf16[64,384]{1,0:T(8,128)(2,1)S(1)}, bf16[64,384]{1,0:T(8,128)(2,1)}, u32[]{:S(2)}) copy-start(bf16[64,384]{1,0:T(8,128)(2,1)} %param.16) | copy-start | bytes 147460
  342.0 6.4 %collective-permute-start = (bf16[180,384]{1,0:T(8,128)(2,1)S(1)}, bf16[180,384]{1,0:T(8,128)(2,1)}, u32[]{:S(2)}, u32[]{:S(2)}) collective-permute-start(bf16[180,384]{1,0:T(8,128)(2,1)S(1)} %slice.81), channel_id=1, source_target_pairs={{0,1},{1,2},{2,3},{3,4},{4,5},{5,6},{6,7},{7,8},{8,9},{9,10},{10,1... | collective-permute-start | bytes 414728
  351.8 3.3 copy-start.11
  351.8 3.3 copy-start.12
  351.8 3.3 copy-start.13
  355.2 76.5 %copy-start.9 = (s32[4]{0:T(128)S(1)}, s32[4]{0:T(128)}, u32[]{:S(2)}) copy-start(s32[4]{0:T(128)} %param.20) | copy-start | bytes 52
  428.2 7.1 %copy-start.1 = (f32[128,128]{1,0:T(8,128)}, f32[128,128]{1,0:T(8,128)S(1)}, u32[]{:S(2)}) copy-start(f32[128,128]{1,0:T(8,128)S(1)} %get-tuple-element.58) | copy-start | bytes 196612
  428.2 7.1 %copy-start.2 = (f32[128,128]{1,0:T(8,128)}, f32[128,128]{1,0:T(8,128)S(1)}, u32[]{:S(2)}) copy-start(f32[128,128]{1,0:T(8,128)S(1)} %get-tuple-element.59) | copy-start | bytes 196612
  428.2 7.1 %copy-start.3 = (f32[16,64,128]{2,1,0:T(8,128)S(1)}, f32[16,64,128]{2,1,0:T(8,128)}, u32[]{:S(2)}) copy-start(f32[16,64,128]{2,1,0:T(8,128)} %fusion.23) | copy-start | bytes 1572868
